TPU v7x, 32 devices: a whole 2x2x4 slice. The times are simulated.
32 devices in a mesh: gx: 4 (over y, x), gy: 8 (over z, core).
Axes of the slice: x: 2, y: 2, z: 4, core: 2. Of those that a mesh axis runs over, the one named last changes fastest.
Arguments:
- source: bfloat16 [288, 4, 8, 1024], P(None, 'gx', 'gy'), may hold values from -6 to 6
- slope: float32 [2, 144], replicated, may hold values from -6 to 6
- quad: bfloat16 [4, 4, 2, 20736], replicated, may hold values from -1 to 1, as said below
- pair: bfloat16 [2, 2, 2, 20736], replicated, may hold values from -1 to 1, as said below
Outputs:
- image: bfloat16 [288, 4, 8, 1024], P(None, 'gx', 'gy')
Inputs may be any that keep to these rules, and one draw needn't show every extreme that they name: `quad`: translation coefficients. `pair`: translation coefficients.
All inputs are finite; a program needn't handle non-finite values.
Results may differ from a plain program's by a relative error of at most 0.02.
Values may be sent and summed in bfloat16 or wider, within the bound.
A program may use at most 64 MiB of HBM per device.

v0:
```python
import functools
import jax
import jax.numpy as jnp
import numpy as np
from jax import lax
from jax.experimental import pallas as pl
from jax.experimental.pallas import tpu as pltpu
from jax.sharding import PartitionSpec as P

P_SIZE = 144
SIDE = 32


def partner(value, axis, stride):
    mask = 2**stride
    pairs = [(source, source ^ mask) for source in range(lax.axis_size(axis))]
    return lax.ppermute(value, axis, pairs)


def complex_block(coefficients):
    real_part = coefficients[..., 0, :, :]
    imag_part = coefficients[..., 1, :, :]
    upper_rows = jnp.concatenate([real_part, -imag_part], -1)
    lower_rows = jnp.concatenate([imag_part, real_part], -1)
    return jnp.concatenate([upper_rows, lower_rows], -2)


def translate(neighbours, mode_x, mode_y, depth, target_x, target_y, quad_block, pair_block):
    width_all, boxes_x, boxes_y = neighbours[0, 0].shape
    split_x = 2 if mode_x == "local" else 1
    inner_x = 1 << depth if mode_x == "local" else 1
    split_y = 2 if mode_y == "local" else 1
    inner_y = 1 << depth if mode_y == "local" else 1
    shape_seven = (
        width_all,
        boxes_x // (split_x * inner_x),
        split_x,
        inner_x,
        boxes_y // (split_y * inner_y),
        split_y,
        inner_y,
    )
    shaped = {}
    for source_key in neighbours:
        shaped[source_key] = neighbours[source_key].reshape(shape_seven)
    steps_x = [0, 1] if mode_x != "none" else [0]
    steps_y = [0, 1]
    stacked_rows = []
    for slot_x in range(split_x):
        columns = []
        for slot_y in range(split_y):
            chosen_x = slot_x if mode_x == "local" else target_x
            chosen_y = slot_y if mode_y == "local" else target_y
            summed = None
            for step_x in steps_x:
                for step_y in steps_y:
                    source_key = (
                        step_x if mode_x == "device" else 0,
                        step_y if mode_y == "device" else 0,
                    )
                    from_x = (slot_x + step_x) % 2 if mode_x == "local" else 0
                    from_y = (slot_y + step_y) % 2 if mode_y == "local" else 0
                    block_rows = shaped[source_key][:, :, from_x, :, :, from_y, :]
                    child_x = (chosen_x + step_x) % 2
                    child_y = (chosen_y + step_y) % 2
                    if mode_x == "none":
                        matrix = pair_block[chosen_y, child_y]
                    else:
                        matrix = quad_block[chosen_x * 2 + chosen_y, child_x * 2 + child_y]
                    product_term = jnp.dot(
                        matrix,
                        block_rows.reshape(width_all, -1),
                        preferred_element_type=jnp.float32,
                    )
                    summed = product_term if summed is None else summed + product_term
            columns.append(summed.reshape(block_rows.shape))
        stacked_rows.append(jnp.stack(columns, 4))
    return jnp.stack(stacked_rows, 2).reshape(width_all, boxes_x, boxes_y)


def rotate(merged, cosine_table, sine_table):
    half_width = merged.shape[0] // 2
    real_part = merged[:half_width]
    imag_part = merged[half_width:]
    return jnp.concatenate(
        [
            real_part * cosine_table - imag_part * sine_table,
            real_part * sine_table + imag_part * cosine_table,
        ],
        0,
    ).astype(jnp.bfloat16)


def local(source, slope, quad, pair):
    width_all = source.shape[0]
    boxes_x = SIDE
    boxes_y = SIDE
    count_x = lax.axis_size("gx")
    count_y = lax.axis_size("gy")
    local_bits_x = boxes_x.bit_length() - 1
    local_bits_y = boxes_y.bit_length() - 1
    device_bits_x = count_x.bit_length() - 1
    device_bits_y = count_y.bit_length() - 1
    levels_x = local_bits_x + device_bits_x
    levels_y = local_bits_y + device_bits_y
    place_x = lax.axis_index("gx")
    place_y = lax.axis_index("gy")
    quad_block = complex_block(quad.reshape(4, 4, 2, P_SIZE, P_SIZE))
    pair_block = complex_block(pair.reshape(2, 2, 2, P_SIZE, P_SIZE))
    center_x = ((place_x * boxes_x + jnp.arange(boxes_x)).astype(jnp.float32) + 0.5) / float(
        boxes_x * count_x
    ) - 0.5
    center_y = ((place_y * boxes_y + jnp.arange(boxes_y)).astype(jnp.float32) + 0.5) / float(
        boxes_y * count_y
    ) - 0.5
    angle = (
        slope[0][:, None, None] * center_x[None, :, None]
        + slope[1][:, None, None] * center_y[None, None, :]
    )
    cosine_table = jnp.cos(angle)
    sine_table = jnp.sin(angle)
    current = source.reshape(width_all, boxes_x, boxes_y)
    last_level = max(levels_x, levels_y)
    for depth in range(last_level):
        mode_x = "local" if depth < local_bits_x else "device" if depth < levels_x else "none"
        mode_y = "local" if depth < local_bits_y else "device"
        neighbours = {(0, 0): current}
        target_x = 0
        target_y = 0
        if mode_x == "device":
            shift_x = depth - local_bits_x
            shift_y = depth - local_bits_y
            target_x = place_x // (1 << shift_x) % 2
            target_y = place_y // (1 << shift_y) % 2
            across_x = partner(current, "gx", shift_x)
            paired = partner(jnp.stack([current, across_x]), "gy", shift_y)
            across_y = paired[0]
            across_both = paired[1]
            neighbours[1, 0] = across_x
            neighbours[0, 1] = across_y
            neighbours[1, 1] = across_both
        elif mode_y == "device":
            shift_y = depth - local_bits_y
            target_y = place_y // (1 << shift_y) % 2
            neighbours[0, 1] = partner(current, "gy", shift_y)
        merged = translate(
            neighbours, mode_x, mode_y, depth, target_x, target_y, quad_block, pair_block
        )
        current = rotate(merged, cosine_table, sine_table)
    return current.reshape(width_all, 1, 1, boxes_x * boxes_y)

LANES = 128
CHIPS = 16
BF16 = jnp.bfloat16
F32 = jnp.float32
MESH_ID = pl.DeviceIdType.MESH


def plan():
    slots = [("i", 4), ("i", 3), ("i", 2)]
    lanes = {64: ("i", 1), 32: ("i", 0)}
    for bit in range(5):
        lanes[1 << bit] = ("j", bit)
    steps = []
    for level in range(5):
        swaps = []
        need = [("i", level), ("j", level)]
        for bit in need:
            if bit in slots:
                continue
            stride = [s for s in lanes if lanes[s] == bit][0]
            free = [k for k in range(3) if slots[k] not in need]
            slot = free[0]
            swaps.append((slot, stride))
            slots[slot], lanes[stride] = lanes[stride], slots[slot]
        steps.append((swaps, slots.index(need[0]), slots.index(need[1])))
    return steps, slots, lanes


STEPS, END_SLOTS, END_LANES = plan()


def home_columns():
    columns = np.zeros(1024, np.int64)
    for place in range(1024):
        block, lane = place // LANES, place % LANES
        values = {END_SLOTS[k]: block >> (2 - k) & 1 for k in range(3)}
        for stride in END_LANES:
            values[END_LANES[stride]] = 1 if lane & stride else 0
        i = sum(values["i", b] << b for b in range(5))
        j = sum(values["j", b] << b for b in range(5))
        columns[place] = i * 32 + j
    return columns


def swap_pair(first, second, stride):
    mask = (lax.broadcasted_iota(jnp.int32, first.shape, 1) & stride) == 0
    low = jnp.where(mask, first, pltpu.roll(second, stride, 1))
    high = jnp.where(mask, pltpu.roll(first, LANES - stride, 1), second)
    return low, high


def slot_index(bits):
    return bits[0] * 4 + bits[1] * 2 + bits[2]


def turn(merged, cosine, sine):
    real_part, imag_part = merged[:P_SIZE], merged[P_SIZE:]
    return jnp.concatenate(
        [real_part * cosine - imag_part * sine, real_part * sine + imag_part * cosine], 0
    ).astype(BF16)


def near_kernel(source_ref, table_ref, weight_ref, out_ref, table_out, state):
    width = 2 * P_SIZE
    for block in range(8):
        columns = pl.ds(block * LANES, LANES)
        state[block, 0:width, :] = source_ref[:, columns]
        state[block, width : 2 * width, :] = table_ref[:, columns]
    for swaps, slot_x, slot_y in STEPS:
        for slot, stride in swaps:
            mask = 4 >> slot
            for block in range(8):
                if not block & mask:
                    low, high = swap_pair(state[block], state[block | mask], stride)
                    state[block] = low
                    state[block | mask] = high
        rest = 3 - slot_x - slot_y

        def at(tx, ty, g):
            bits = [0, 0, 0]
            bits[slot_x], bits[slot_y], bits[rest] = tx, ty, g
            return slot_index(bits)

        stacked = jnp.concatenate(
            [
                jnp.concatenate([state[at(c // 2, c % 2, g), 0:width, :] for g in range(2)], 1)
                for c in range(4)
            ],
            0,
        )
        for t in range(4):
            merged = jnp.dot(
                weight_ref[t * width : (t + 1) * width, :], stacked, preferred_element_type=F32
            )
            for g in range(2):
                block = at(t // 2, t % 2, g)
                table = state[block, width : 2 * width, :].astype(F32)
                state[block, 0:width, :] = turn(
                    merged[:, g * LANES : (g + 1) * LANES], table[:P_SIZE], table[P_SIZE:]
                )
    for block in range(8):
        low, high = swap_pair(
            state[block, 0:P_SIZE, :], state[block, P_SIZE:width, :], 64
        )
        out_ref[2 * block] = low
        out_ref[2 * block + 1] = high
        table_out[block] = state[block, width : 2 * width, :]


def far_kernel(own_ref, table_ref, shift_ref, weight_ref, pair_ref, out_ref, state, tables, other):
    width = 2 * P_SIZE
    half = lax.axis_index("gy") // 2 % 2
    chip = lax.axis_index("gx") * 4 + lax.axis_index("gy") // 2
    core = lax.axis_index("gy") % 2
    lane = lax.broadcasted_iota(jnp.int32, (P_SIZE, LANES), 1)
    keep = (lane // 64) == half
    table = table_ref[chip // 2].astype(F32)
    base = []
    for k in range(2):
        part = table[k * P_SIZE : (k + 1) * P_SIZE]
        base.append(jnp.where(keep, part, pltpu.roll(part, 64, 1)))

    def chip_of(y, x, z1, z0):
        return y * 8 + x * 4 + z1 * 2 + z0

    for y in range(2):
        for x in range(2):
            for z0 in range(2):
                block = y * 4 + x * 2 + z0
                pick = []
                for k in range(2):
                    low = shift_ref[k, :, chip_of(y, x, 0, z0) : chip_of(y, x, 0, z0) + 1]
                    high = shift_ref[k, :, chip_of(y, x, 1, z0) : chip_of(y, x, 1, z0) + 1]
                    pick.append(jnp.where(lane < 64, low, high))
                tables[block, 0] = base[0] * pick[0] - base[1] * pick[1]
                tables[block, 1] = base[0] * pick[1] + base[1] * pick[0]
                for step in range(2):
                    low, high = swap_pair(
                        own_ref[step, chip_of(y, x, 0, z0)], own_ref[step, chip_of(y, x, 1, z0)], 64
                    )
                    target = state if step == 0 else other
                    target[block, 0:P_SIZE, :] = low
                    target[block, P_SIZE:width, :] = high

    def emit(merged, blocks):
        for n, block in enumerate(blocks):
            state[block] = turn(
                merged[:, n * LANES : (n + 1) * LANES], tables[block, 0], tables[block, 1]
            )

    groups = [(y, z0) for y in range(2) for z0 in range(2)]
    stacked = jnp.concatenate(
        [
            jnp.concatenate([ref[y * 4 + x * 2 + z0] for y, z0 in groups], 1)
            for x in range(2)
            for ref in (state, other)
        ],
        0,
    )
    is_first = core == 0
    swapped = []
    for x in range(2):
        mine = stacked[(2 * x) * width : (2 * x + 1) * width]
        theirs = stacked[(2 * x + 1) * width : (2 * x + 2) * width]
        swapped += [jnp.where(is_first, mine, theirs), jnp.where(is_first, theirs, mine)]
    stacked = jnp.concatenate(swapped, 0)
    for x in range(2):
        row = pl.multiple_of((x * 2 + core) * width, width)
        merged = jnp.dot(
            weight_ref[pl.ds(row, width), :], stacked, preferred_element_type=F32
        )
        emit(merged, [y * 4 + x * 2 + z0 for y, z0 in groups])
    stacked = jnp.concatenate(
        [
            jnp.concatenate([state[c // 2 * 4 + x * 2 + c % 2] for x in range(2)], 1)
            for c in range(4)
        ],
        0,
    )
    for t in range(4):
        merged = jnp.dot(
            weight_ref[t * width : (t + 1) * width, :], stacked, preferred_element_type=F32
        )
        emit(merged, [t // 2 * 4 + x * 2 + t % 2 for x in range(2)])
    for block in range(4):
        low, high = swap_pair(state[block], state[block + 4], 64)
        state[block] = low
        state[block + 4] = high
        for k in range(2):
            low, high = swap_pair(tables[block, k], tables[block + 4, k], 64)
            tables[block, k] = low
            tables[block + 4, k] = high
    stacked = jnp.concatenate(
        [jnp.concatenate([state[c * 4 + g] for g in range(4)], 1) for c in range(2)], 0
    )
    for t in range(2):
        merged = jnp.dot(
            pair_ref[t * width : (t + 1) * width, :], stacked, preferred_element_type=F32
        )
        emit(merged, [t * 4 + g for g in range(4)])
    for z1 in range(2):
        for x in range(2):
            for z0 in range(2):
                block = z1 * 4 + x * 2 + z0
                low, high = swap_pair(
                    state[block, 0:P_SIZE, :], state[block, P_SIZE:width, :], 64
                )
                out_ref[chip_of(0, x, z1, z0)] = low
                out_ref[chip_of(1, x, z1, z0)] = high


def home_kernel(block_ref, order_ref, out_ref, state):
    for block in range(8):
        low, high = swap_pair(block_ref[2 * block], block_ref[2 * block + 1], 64)
        columns = slice(block * LANES, (block + 1) * LANES)
        state[0:P_SIZE, columns] = low
        state[P_SIZE : 2 * P_SIZE, columns] = high
    for part in range(4):
        columns = slice(part * 256, (part + 1) * 256)
        out_ref[:, columns] = jnp.dot(
            state[...], order_ref[:, columns], preferred_element_type=F32
        ).astype(BF16)


def trade_kernel(both, in_ref, out_ref, send_sem, recv_sem, pass_send, pass_recv, own_sem):
    gx = lax.axis_index("gx")
    gy = lax.axis_index("gy")
    core = gy % 2
    chip = gx * 4 + gy // 2
    mate = (gx, gy // 2 * 2 + (1 - core))

    def place(index):
        return (index // 4, index % 4 * 2 + core)

    barrier = pltpu.get_barrier_semaphore()
    for k in range(1, CHIPS):
        pl.semaphore_signal(
            barrier, inc=1, device_id=place((chip + k) % CHIPS), device_id_type=MESH_ID
        )
    if both:
        pl.semaphore_signal(barrier, inc=1, device_id=mate, device_id_type=MESH_ID)
    pl.semaphore_wait(barrier, CHIPS if both else CHIPS - 1)

    def landing(which, index):
        return out_ref.at[which, index] if both else out_ref.at[index]

    sends = []
    for k in range(1, CHIPS):
        dest = (chip + k) % CHIPS
        copy = pltpu.make_async_remote_copy(
            src_ref=in_ref.at[dest],
            dst_ref=landing(0, chip),
            send_sem=send_sem.at[k],
            recv_sem=recv_sem.at[k],
            device_id=place(dest),
            device_id_type=MESH_ID,
        )
        copy.start()
        sends.append(copy)
    own = pltpu.make_async_copy(in_ref.at[chip], landing(0, chip), own_sem)
    own.start()

    def forward(k, src):
        index = (chip + CHIPS - k) % CHIPS
        copy = pltpu.make_async_remote_copy(
            src_ref=src,
            dst_ref=landing(1, index),
            send_sem=pass_send.at[k],
            recv_sem=pass_recv.at[k],
            device_id=mate,
            device_id_type=MESH_ID,
        )
        copy.start()
        return copy

    passes = []
    if both:
        passes.append(forward(0, in_ref.at[chip]))
    for k in range(1, CHIPS):
        sends[k - 1].wait_recv()
        if both:
            passes.append(forward(k, landing(0, (chip + CHIPS - k) % CHIPS)))
    own.wait()
    for copy in sends:
        copy.wait_send()
    for copy in passes:
        copy.wait()


def trade(blocks, both, identity):
    shape = ((2,) if both else ()) + blocks.shape
    return pl.pallas_call(
        functools.partial(trade_kernel, both),
        out_shape=jax.ShapeDtypeStruct(shape, BF16),
        in_specs=[pl.BlockSpec(memory_space=pl.ANY)],
        out_specs=pl.BlockSpec(memory_space=pl.ANY),
        scratch_shapes=[pltpu.SemaphoreType.DMA((CHIPS,))] * 4 + [pltpu.SemaphoreType.DMA],
        compiler_params=pltpu.CompilerParams(collective_id=identity, has_side_effects=True),
    )(blocks)


def merged_block(coefficients, count):
    shaped = coefficients.reshape(count, count, 2, P_SIZE, P_SIZE)
    real_part = shaped[:, :, 0].transpose(0, 2, 1, 3)
    imag_part = shaped[:, :, 1].transpose(0, 2, 1, 3)
    upper = jnp.stack([real_part, -imag_part], 3)
    lower = jnp.stack([imag_part, real_part], 3)
    size = count * 2 * P_SIZE
    return jnp.stack([upper, lower], 1).reshape(size, size)


def turned(angle):
    return jnp.cos(angle), jnp.sin(angle)


def traded(source, slope, quad, pair):
    width_all = source.shape[0]
    count_x = lax.axis_size("gx")
    count_y = lax.axis_size("gy")
    place_x = lax.axis_index("gx")
    place_y = lax.axis_index("gy")
    core = place_y % 2
    total_x = float(SIDE * count_x)
    total_y = float(SIDE * count_y)
    steps = jnp.arange(SIDE)
    center_x = ((place_x * SIDE + steps).astype(F32) + 0.5) / total_x - 0.5
    center_y = ((place_y * SIDE + steps).astype(F32) + 0.5) / total_y - 0.5
    tiles = jnp.arange(CHIPS)
    far_x = ((tiles // 4 - place_x) * SIDE).astype(F32) / total_x
    far_y = ((tiles % 4 * 2 + core - place_y) * SIDE).astype(F32) / total_y
    angle = jnp.concatenate(
        [
            slope[0][:, None] * center_x[None],
            slope[1][:, None] * center_y[None],
            slope[0][:, None] * far_x[None] + slope[1][:, None] * far_y[None],
        ],
        1,
    )
    cosine, sine = turned(angle)
    cos_x, sin_x = cosine[:, :SIDE, None], sine[:, :SIDE, None]
    cos_y, sin_y = cosine[:, None, SIDE : 2 * SIDE], sine[:, None, SIDE : 2 * SIDE]
    table = jnp.concatenate([cos_x * cos_y - sin_x * sin_y, cos_x * sin_y + sin_x * cos_y], 0)
    table = table.astype(BF16).reshape(width_all, SIDE * SIDE)
    shift = jnp.stack([cosine[:, 2 * SIDE :], sine[:, 2 * SIDE :]])
    weight = merged_block(quad, 4)
    pair_weight = merged_block(pair, 2)
    order = jnp.asarray(home_columns()[:, None] == np.arange(SIDE * SIDE)[None], BF16)
    roomy = pltpu.CompilerParams(vmem_limit_bytes=50 * 1024 * 1024)
    block_shape = jax.ShapeDtypeStruct((CHIPS, P_SIZE, LANES), BF16)
    blocks, near_table = pl.pallas_call(
        near_kernel,
        out_shape=(block_shape, jax.ShapeDtypeStruct((8, width_all, LANES), BF16)),
        scratch_shapes=[pltpu.VMEM((8, 2 * width_all, LANES), BF16)],
        compiler_params=roomy,
    )(source.reshape(width_all, SIDE * SIDE), table, weight)
    gathered = trade(blocks, True, 0)
    results = pl.pallas_call(
        far_kernel,
        out_shape=block_shape,
        scratch_shapes=[
            pltpu.VMEM((8, width_all, LANES), BF16),
            pltpu.VMEM((8, 2, P_SIZE, LANES), F32),
            pltpu.VMEM((8, width_all, LANES), BF16),
        ],
        compiler_params=roomy,
    )(gathered, near_table, shift, weight, pair_weight)
    returned = trade(results, False, 1)
    image = pl.pallas_call(
        home_kernel,
        out_shape=jax.ShapeDtypeStruct((width_all, SIDE * SIDE), BF16),
        scratch_shapes=[pltpu.VMEM((width_all, SIDE * SIDE), BF16)],
        compiler_params=roomy,
    )(returned, order)
    return image.reshape(width_all, 1, 1, SIDE * SIDE)


def solution(mesh):
    in_specs = (P(None, "gx", "gy", None), P(), P(), P())
    out_specs = P(None, "gx", "gy", None)
    fits = mesh.shape["gx"] == 4 and mesh.shape["gy"] == 8
    body = traded if fits else local
    return jax.shard_map(body, mesh=mesh, in_specs=in_specs, out_specs=out_specs, check_vma=False)
```

profile of v0, /device:TPU:0, one launch (start us, length us, event | category | flops | bytes accessed | tf_op | source)
XLA Modules:
  0.0 105.7 jit_solution(5925131477713378473)
XLA Ops:
  0.0 0.8 fusion.16
  1.3 0.6 copy-done.8
  1.9 0.3 subtract_convert_fusion
  2.7 0.9 copy-done.6
  3.6 1.6 %copy.26 = bf16[4,4,2,20736]{3,1,0,2:T(4,128)(2,1)} copy(bf16[4,4,2,20736]{3,2,1,0:T(2,128)(2,1)S(1)} %copy-done.6) | data formatting | bytes 2654208 | tf_op args[2]
  5.2 4.9 %reshape.92 = bf16[4,4,2,144,144]{4,3,1,0,2:T(8,128)(2,1)S(1)} reshape(bf16[4,4,2,20736]{3,1,0,2:T(4,128)(2,1)} %copy.26) | data formatting | bytes 2654208 | tf_op jit(solution)/shard_map/reshape | solution.py:454
  10.4 0.6 maximum_bitcast_fusion
  11.0 3.1 %pad_maximum_fusion = bf16[4,2,144,4,2,144]{5,2,4,3,0,1:T(8,128)(2,1)} fusion(bf16[4,1,144,4,2,144]{5,2,4,3,0,1:T(8,128)(2,1)S(1)} %get-tuple-element.12, bf16[4,1,144,4,2,144]{5,2,4,3,0,1:T(8,128)(2,1)S(1)} %get-tuple-element.11), kind=kLoop, calls=%fused_computation | loop fusion | flops 1327104 | bytes 5308416 | tf_op jit(solution)/shard_map/stack | solution.py:460
  14.1 8.4 %copy.27 = bf16[4,2,144,4,2,144]{5,4,3,2,1,0:T(2,128)(2,1)} copy(bf16[4,2,144,4,2,144]{5,2,4,3,0,1:T(8,128)(2,1)} %pad_maximum_fusion) | data formatting | bytes 5308416 | tf_op jit(solution)/shard_map/stack | solution.py:460
  22.5 12.0 %reshape.93.weight_ref = bf16[1152,1152]{1,0:T(8,128)(2,1)} reshape(bf16[4,2,144,4,2,144]{5,4,3,2,1,0:T(2,128)(2,1)} %copy.27) | data formatting | bytes 5308416 | tf_op jit(solution)/shard_map/reshape | solution.py:460
  34.5 9.2 %shard_map.55 = (bf16[16,144,128]{2,1,0:T(8,128)(2,1)S(1)}, bf16[8,288,128]{2,1,0:T(8,128)(2,1)S(1)}) custom-call(bf16[288,1024]{1,0:T(8,128)(2,1)S(1)} %bitcast.56, bf16[288,1024]{1,0:T(8,128)(2,1)S(1)} %pad_maximum_fusion.2.table_ref, bf16[1152,1152]{1,0:T(8,128)(2,1)} %reshape.93.weight_ref), custom_call_target="tpu_custom_call" | custom-call | tf_op jit(solution)/shard_map/pallas_call | solution.py:501
  43.7 0.8 copy-done.4
  44.5 22.3 %shard_map.56.own_ref = bf16[2,16,144,128]{3,2,1,0:T(8,128)(2,1)} custom-call(bf16[16,144,128]{2,1,0:T(8,128)(2,1)} %copy-done.4), custom_call_target="tpu_custom_call" | custom-call | tf_op jit(solution)/shard_map/pallas_call | solution.py:443
  66.8 0.7 slice_bitcast_fusion.4
  67.5 0.7 slice_bitcast_fusion.5
  68.7 1.1 %reshape.94 = bf16[2,2,2,144,144]{4,3,1,0,2:T(8,128)(2,1)S(1)} reshape(bf16[2,2,2,20736]{3,1,0,2:T(2,128)(2,1)S(1)} %copy.28) | data formatting | bytes 663552 | tf_op jit(solution)/shard_map/reshape | solution.py:454
  70.3 1.9 %copy.29 = bf16[2,2,144,2,2,144]{5,4,3,2,1,0:T(2,128)(2,1)} copy(bf16[2,2,144,2,2,144]{5,2,4,3,0,1:T(8,128)(2,1)S(1)} %pad_maximum_fusion.1) | data formatting | bytes 1327104 | tf_op jit(solution)/shard_map/stack | solution.py:460
  72.2 4.4 %reshape.95.pair_ref = bf16[576,576]{1,0:T(8,128)(2,1)S(1)} reshape(bf16[2,2,144,2,2,144]{5,4,3,2,1,0:T(2,128)(2,1)} %copy.29) | data formatting | bytes 1327104 | tf_op jit(solution)/shard_map/reshape | solution.py:460
  76.6 5.0 %shard_map.57.in_ref = bf16[16,144,128]{2,1,0:T(8,128)(2,1)S(1)} custom-call(bf16[2,16,144,128]{3,2,1,0:T(8,128)(2,1)S(1)} %copy-done, bf16[8,288,128]{2,1,0:T(8,128)(2,1)S(1)} %get-tuple-element.8.table_ref, f32[2,144,16]{2,1,0:T(8,128)S(1)} %copy.30.shift_ref, bf16[1152,1152]{1,0:T(8,128)(2,1)} %reshape.93.weight_ref, bf16[576,576]{1,0:T(8,128)(2,1)S(1)} %reshape.95.pair_ref), custom_call_target="tpu_custom_call" | custom-call | tf_op jit(solution)/shard_map/pallas_call | solution.py:508
  81.6 0.8 copy-done.1
  82.4 19.0 %shard_map.58.block_ref = bf16[16,144,128]{2,1,0:T(8,128)(2,1)} custom-call(bf16[16,144,128]{2,1,0:T(8,128)(2,1)} %copy-done.1), custom_call_target="tpu_custom_call" | custom-call | tf_op jit(solution)/shard_map/pallas_call | solution.py:443
  101.4 1.1 copy-done.2
  102.4 1.6 %copy-done.3 = bf16[1024,1024]{1,0:T(8,128)(2,1)S(1)} copy-done((bf16[1024,1024]{1,0:T(8,128)(2,1)S(1)}, bf16[1024,1024]{1,0:T(8,128)(2,1)}, u32[]{:S(2)}) %copy-start.3) | copy-done | bytes 2097176
  104.0 1.7 %shard_map.59 = bf16[288,1024]{1,0:T(8,128)(2,1)} custom-call(bf16[16,144,128]{2,1,0:T(8,128)(2,1)S(1)} %copy-done.2, bf16[1024,1024]{1,0:T(8,128)(2,1)S(1)} %copy-done.3), custom_call_target="tpu_custom_call" | custom-call | tf_op jit(solution)/shard_map/pallas_call | solution.py:519
  (34 shorter events, 2.1 us)
Async XLA Ops:
  1.2 0.6 copy-start.8
  1.3 0.7 copy-start.9
  2.3 1.3 %copy-start.6 = (bf16[4,4,2,20736]{3,2,1,0:T(2,128)(2,1)S(1)}, bf16[4,4,2,20736]{3,2,1,0:T(2,128)(2,1)}, u32[]{:S(2)}) copy-start(bf16[4,4,2,20736]{3,2,1,0:T(2,128)(2,1)} %param.7) | copy-start | bytes 3981316
  22.5 12.0 %copy-start.5 = (bf16[288,1,1,1024]{3,0,2,1:T(8,128)(2,1)S(1)}, bf16[288,1,1,1024]{3,0,2,1:T(8,128)(2,1)}, u32[]{:S(2)}) copy-start(bf16[288,1,1,1024]{3,0,2,1:T(8,128)(2,1)} %param.5) | copy-start | bytes 1769476
  43.7 0.8 copy-start.4
  44.5 23.8 %copy-start.7 = (bf16[2,2,2,20736]{3,2,1,0:T(2,128)(2,1)S(1)}, bf16[2,2,2,20736]{3,2,1,0:T(2,128)(2,1)}, u32[]{:S(2)}) copy-start(bf16[2,2,2,20736]{3,2,1,0:T(2,128)(2,1)} %param.8) | copy-start | bytes 995332
  72.2 4.4 %copy-start = (bf16[2,16,144,128]{3,2,1,0:T(8,128)(2,1)S(1)}, bf16[2,16,144,128]{3,2,1,0:T(8,128)(2,1)}, u32[]{:S(2)}) copy-start(bf16[2,16,144,128]{3,2,1,0:T(8,128)(2,1)} %shard_map.56.own_ref) | copy-start | bytes 3538948
  81.6 0.8 copy-start.1
  101.4 1.1 %copy-start.2 = (bf16[16,144,128]{2,1,0:T(8,128)(2,1)S(1)}, bf16[16,144,128]{2,1,0:T(8,128)(2,1)}, u32[]{:S(2)}) copy-start(bf16[16,144,128]{2,1,0:T(8,128)(2,1)} %shard_map.58.block_ref) | copy-start | bytes 1769476
  102.4 1.6 %copy-start.3 = (bf16[1024,1024]{1,0:T(8,128)(2,1)S(1)}, bf16[1024,1024]{1,0:T(8,128)(2,1)}, u32[]{:S(2)}) copy-start(bf16[1024,1024]{1,0:T(8,128)(2,1)} %constant.70.clone.order_ref) | copy-start | bytes 6291460
where the time goes:
time: 106 us
  Pallas kernels  57.1 us (54%)
  local copies, waits for them, and re-layouts  43.3 us (41%)
  other arithmetic  5.12 us (5%)
    pallas_call x2, Pallas kernels, trade(): pl.pallas_call(functools.partial(trade_kernel, both), out_shape=jax.Shape...  41.3 us
    reshape x2, local copies, waits for them, and re-layouts, merged_block(): return jnp.stack([upper, lower], 1).reshape(size, size)  16.4 us
    another operation x2, local copies, waits for them, and re-layouts, merged_block(): return jnp.stack([upper, lower], 1).reshape(size, size)  10.3 us
    pallas_call x1, Pallas kernels, traded(): pl.pallas_call(near_kernel, out_shape=(block_shape, jax.ShapeDtypeStruct(...  9.18 us
    unnamed x22, local copies, waits for them, and re-layouts  7.66 us
    reshape x2, local copies, waits for them, and re-layouts, merged_block(): shaped = coefficients.reshape(count, count, 2, P_SIZE, P_SIZE)  5.96 us
    pallas_call x1, Pallas kernels, traded(): pl.pallas_call(far_kernel, out_shape=block_shape, scratch_shapes=[pltpu.V...  4.98 us
    another operation x4, other arithmetic, merged_block(): return jnp.stack([upper, lower], 1).reshape(size, size)  4.15 us

commit v1 on v0

--- a/solution.py
+++ b/solution.py
@@ -211,8 +211,40 @@
     ).astype(BF16)
 
 
-def near_kernel(source_ref, table_ref, weight_ref, out_ref, table_out, state):
+def assemble(matrix_ref, weight_ref, count):
+    kept = count * 2 * LANES
+    for t in range(count):
+        parts = [
+            [matrix_ref[(t * count + c) * 2 + r] for r in range(2)] for c in range(count)
+        ]
+        for out in range(2):
+            rows = slice((t * 2 + out) * P_SIZE, (t * 2 + out + 1) * P_SIZE)
+            rests = []
+            for c in range(count):
+                for side in range(2):
+                    piece = parts[c][out ^ side]
+                    if side == 1 and out == 0:
+                        piece = -piece
+                    first = (c * 2 + side) * LANES
+                    weight_ref[rows, first : first + LANES] = piece[:, :LANES]
+                    rests.append(piece[:, LANES:])
+            weight_ref[rows, kept : kept + 16 * len(rests)] = jnp.concatenate(rests, 1)
+
+
+def stack_children(children):
+    mains = []
+    rests = []
+    for child in children:
+        for side in range(2):
+            first = side * P_SIZE
+            mains.append(child[first : first + LANES])
+            rests.append(child[first + LANES : first + P_SIZE])
+    return jnp.concatenate(mains + rests, 0)
+
+
+def near_kernel(source_ref, table_ref, matrix_ref, out_ref, table_out, weight_ref, state):
     width = 2 * P_SIZE
+    assemble(matrix_ref, weight_ref, 4)
     for block in range(8):
         columns = pl.ds(block * LANES, LANES)
         state[block, 0:width, :] = source_ref[:, columns]
@@ -232,12 +264,11 @@
             bits[slot_x], bits[slot_y], bits[rest] = tx, ty, g
             return slot_index(bits)
 
-        stacked = jnp.concatenate(
+        stacked = stack_children(
             [
                 jnp.concatenate([state[at(c // 2, c % 2, g), 0:width, :] for g in range(2)], 1)
                 for c in range(4)
-            ],
-            0,
+            ]
         )
         for t in range(4):
             merged = jnp.dot(
@@ -258,8 +289,11 @@
         table_out[block] = state[block, width : 2 * width, :]
 
 
-def far_kernel(own_ref, table_ref, shift_ref, weight_ref, pair_ref, out_ref, state, tables, other):
+def far_kernel(
+    own_ref, table_ref, shift_ref, weight_ref, matrix_ref, out_ref, state, tables, other, pair_ref
+):
     width = 2 * P_SIZE
+    assemble(matrix_ref, pair_ref, 2)
     half = lax.axis_index("gy") // 2 % 2
     chip = lax.axis_index("gx") * 4 + lax.axis_index("gy") // 2
     core = lax.axis_index("gy") % 2
@@ -300,33 +334,26 @@
             )
 
     groups = [(y, z0) for y in range(2) for z0 in range(2)]
-    stacked = jnp.concatenate(
-        [
+    is_first = core == 0
+    children = []
+    for x in range(2):
+        mine, theirs = [
             jnp.concatenate([ref[y * 4 + x * 2 + z0] for y, z0 in groups], 1)
-            for x in range(2)
             for ref in (state, other)
-        ],
-        0,
-    )
-    is_first = core == 0
-    swapped = []
-    for x in range(2):
-        mine = stacked[(2 * x) * width : (2 * x + 1) * width]
-        theirs = stacked[(2 * x + 1) * width : (2 * x + 2) * width]
-        swapped += [jnp.where(is_first, mine, theirs), jnp.where(is_first, theirs, mine)]
-    stacked = jnp.concatenate(swapped, 0)
+        ]
+        children += [jnp.where(is_first, mine, theirs), jnp.where(is_first, theirs, mine)]
+    stacked = stack_children(children)
     for x in range(2):
         row = pl.multiple_of((x * 2 + core) * width, width)
         merged = jnp.dot(
             weight_ref[pl.ds(row, width), :], stacked, preferred_element_type=F32
         )
         emit(merged, [y * 4 + x * 2 + z0 for y, z0 in groups])
-    stacked = jnp.concatenate(
+    stacked = stack_children(
         [
             jnp.concatenate([state[c // 2 * 4 + x * 2 + c % 2] for x in range(2)], 1)
             for c in range(4)
-        ],
-        0,
+        ]
     )
     for t in range(4):
         merged = jnp.dot(
@@ -341,8 +368,8 @@
             low, high = swap_pair(tables[block, k], tables[block + 4, k], 64)
             tables[block, k] = low
             tables[block + 4, k] = high
-    stacked = jnp.concatenate(
-        [jnp.concatenate([state[c * 4 + g] for g in range(4)], 1) for c in range(2)], 0
+    stacked = stack_children(
+        [jnp.concatenate([state[c * 4 + g] for g in range(4)], 1) for c in range(2)]
     )
     for t in range(2):
         merged = jnp.dot(
@@ -395,9 +422,18 @@
     def landing(which, index):
         return out_ref.at[which, index] if both else out_ref.at[index]
 
+    far_first = [(1, a, b) for a in range(4) for b in range(2)]
+    far_first += [(0, a, b) for a in range(4) for b in range(2) if a or b]
+    zed = gy // 2
+
+    def across(hop, back):
+        other_half, a, b = hop
+        x = (gx + (4 - a if back else a)) % 4
+        return x * 4 + (zed // 2 + other_half) % 2 * 2 + (zed + b) % 2
+
     sends = []
     for k in range(1, CHIPS):
-        dest = (chip + k) % CHIPS
+        dest = across(far_first[k - 1], False)
         copy = pltpu.make_async_remote_copy(
             src_ref=in_ref.at[dest],
             dst_ref=landing(0, chip),
@@ -412,7 +448,7 @@
     own.start()
 
     def forward(k, src):
-        index = (chip + CHIPS - k) % CHIPS
+        index = across(far_first[k - 1], True) if k else chip
         copy = pltpu.make_async_remote_copy(
             src_ref=src,
             dst_ref=landing(1, index),
@@ -430,7 +466,7 @@
     for k in range(1, CHIPS):
         sends[k - 1].wait_recv()
         if both:
-            passes.append(forward(k, landing(0, (chip + CHIPS - k) % CHIPS)))
+            passes.append(forward(k, landing(0, across(far_first[k - 1], True))))
     own.wait()
     for copy in sends:
         copy.wait_send()
@@ -448,16 +484,6 @@
         scratch_shapes=[pltpu.SemaphoreType.DMA((CHIPS,))] * 4 + [pltpu.SemaphoreType.DMA],
         compiler_params=pltpu.CompilerParams(collective_id=identity, has_side_effects=True),
     )(blocks)
-
-
-def merged_block(coefficients, count):
-    shaped = coefficients.reshape(count, count, 2, P_SIZE, P_SIZE)
-    real_part = shaped[:, :, 0].transpose(0, 2, 1, 3)
-    imag_part = shaped[:, :, 1].transpose(0, 2, 1, 3)
-    upper = jnp.stack([real_part, -imag_part], 3)
-    lower = jnp.stack([imag_part, real_part], 3)
-    size = count * 2 * P_SIZE
-    return jnp.stack([upper, lower], 1).reshape(size, size)
 
 
 def turned(angle):
@@ -493,17 +519,21 @@
     table = jnp.concatenate([cos_x * cos_y - sin_x * sin_y, cos_x * sin_y + sin_x * cos_y], 0)
     table = table.astype(BF16).reshape(width_all, SIDE * SIDE)
     shift = jnp.stack([cosine[:, 2 * SIDE :], sine[:, 2 * SIDE :]])
-    weight = merged_block(quad, 4)
-    pair_weight = merged_block(pair, 2)
+    matrices = quad.reshape(32, P_SIZE, P_SIZE)
+    pairs = pair.reshape(8, P_SIZE, P_SIZE)
     order = jnp.asarray(home_columns()[:, None] == np.arange(SIDE * SIDE)[None], BF16)
     roomy = pltpu.CompilerParams(vmem_limit_bytes=50 * 1024 * 1024)
     block_shape = jax.ShapeDtypeStruct((CHIPS, P_SIZE, LANES), BF16)
-    blocks, near_table = pl.pallas_call(
+    blocks, near_table, weight = pl.pallas_call(
         near_kernel,
-        out_shape=(block_shape, jax.ShapeDtypeStruct((8, width_all, LANES), BF16)),
+        out_shape=(
+            block_shape,
+            jax.ShapeDtypeStruct((8, width_all, LANES), BF16),
+            jax.ShapeDtypeStruct((4 * width_all, 4 * width_all), BF16),
+        ),
         scratch_shapes=[pltpu.VMEM((8, 2 * width_all, LANES), BF16)],
         compiler_params=roomy,
-    )(source.reshape(width_all, SIDE * SIDE), table, weight)
+    )(source.reshape(width_all, SIDE * SIDE), table, matrices)
     gathered = trade(blocks, True, 0)
     results = pl.pallas_call(
         far_kernel,
@@ -512,9 +542,10 @@
             pltpu.VMEM((8, width_all, LANES), BF16),
             pltpu.VMEM((8, 2, P_SIZE, LANES), F32),
             pltpu.VMEM((8, width_all, LANES), BF16),
+            pltpu.VMEM((2 * width_all, 2 * width_all), BF16),
         ],
         compiler_params=roomy,
-    )(gathered, near_table, shift, weight, pair_weight)
+    )(gathered, near_table, shift, weight, pairs)
     returned = trade(results, False, 1)
     image = pl.pallas_call(
         home_kernel,

time: 106 us -> 72.4 us (0.68)
  local copies, waits for them, and re-layouts: 43.3 us -> 13.1 us
  other arithmetic: 5.12 us -> 0.87 us
    reshape x4 -> x2, local copies, waits for them, and re-layouts: 22.3 us -> 6.66 us  [the longest x1 5.58 us: traded(): matrices = quad.reshape(32, P_SIZE, P_SIZE)]
    another operation x4 -> x0, local copies, waits for them, and re-layouts: 10.6 us -> none  [the longest x2 10.3 us: merged_block(): return jnp.stack([upper, lower], 1).reshape(size, size)]
    another operation x7 -> x1, other arithmetic: 4.6 us -> 0.35 us  [the longest x4 4.15 us: merged_block(): return jnp.stack([upper, lower], 1).reshape(size, size)]
    unnamed x22 -> x16, local copies, waits for them, and re-layouts: 7.66 us -> 5.21 us
    another operation x3, local copies, waits for them, and re-layouts: 1.54 us -> 0.11 us  [traded(): shift = jnp.stack([cosine[:, 2 * SIDE:], sine[:, 2 * SIDE:]])]
where the time goes in v1:
time: 72.4 us; the launch traced here: 72 us
  Pallas kernels  57.9 us (80%)
  local copies, waits for them, and re-layouts  13.1 us (18%)
  other arithmetic  0.87 us (1%)
    pallas_call x2, Pallas kernels, trade(): pl.pallas_call(functools.partial(trade_kernel, both), out_shape=jax.Shape...  41.6 us
    pallas_call x1, Pallas kernels, traded(): pl.pallas_call(near_kernel, out_shape=(block_shape, jax.ShapeDtypeStruct(...  9.57 us
    reshape x1, local copies, waits for them, and re-layouts, traded(): matrices = quad.reshape(32, P_SIZE, P_SIZE)  5.58 us
    unnamed x16, local copies, waits for them, and re-layouts  5.21 us
    pallas_call x1, Pallas kernels, traded(): pl.pallas_call(far_kernel, out_shape=block_shape, scratch_shapes=[pltpu.V...  5.09 us
    pallas_call x1, Pallas kernels, traded(): pl.pallas_call(home_kernel, out_shape=jax.ShapeDtypeStruct((width_all, SI...  1.66 us

profile of v1, /device:TPU:0, one launch (start us, length us, event | category | flops | bytes accessed | tf_op | source)
XLA Modules:
  0.0 72.0 jit_solution(15203633407417923922)
XLA Ops:
  0.0 0.8 %fusion.14 = (f32[1,144]{1,0:T(1,128)S(1)}, f32[1,144]{1,0:T(1,128)S(1)}) fusion(f32[2,144]{1,0:T(2,128)} %param.6), kind=kLoop, calls=%fused_computation.31 | loop fusion | bytes 2304 | tf_op jit(solution)/shard_map/slice | solution.py:510
  0.8 0.1 multiply_add_fusion
  0.9 0.1 broadcast_multiply_fusion
  0.9 0.3 fusion.1
  1.3 0.3 subtract_convert_fusion
  1.6 0.0 copy-start.6
  1.6 0.2 copy.12
  1.8 0.2 copy.13
  2.0 0.9 %copy-done.6 = bf16[4,4,2,20736]{3,2,1,0:T(2,128)(2,1)S(1)} copy-done((bf16[4,4,2,20736]{3,2,1,0:T(2,128)(2,1)S(1)}, bf16[4,4,2,20736]{3,2,1,0:T(2,128)(2,1)}, u32[]{:S(2)}) %copy-start.6) | copy-done | bytes 1327128
  3.0 5.6 %reshape.86.matrix_ref = bf16[32,144,144]{2,1,0:T(8,128)(2,1)} reshape(bf16[4,4,2,20736]{3,2,1,0:T(2,128)(2,1)S(1)} %copy-done.6) | data formatting | bytes 2654208 | tf_op jit(solution)/shard_map/reshape | solution.py:522
  8.5 9.6 %shard_map.55 = (bf16[16,144,128]{2,1,0:T(8,128)(2,1)S(1)}, bf16[8,288,128]{2,1,0:T(8,128)(2,1)S(1)}, bf16[1152,1152]{1,0:T(8,128)(2,1)}) custom-call(bf16[288,1024]{1,0:T(8,128)(2,1)S(1)} %bitcast.10, bf16[288,1024]{1,0:T(8,128)(2,1)S(1)} %pad_maximum_fusion.table_ref, bf16[32,144,144]{2,1,0:T(8,128)(2,1)} %reshape.86.matrix_ref), custom_call_target="tpu_custom_call" | custom-call | tf_op jit(solution)/shard_map/pallas_call | solution.py:527
  18.1 0.0 copy-start.5
  18.1 0.8 %copy-done.5 = bf16[16,144,128]{2,1,0:T(8,128)(2,1)} copy-done((bf16[16,144,128]{2,1,0:T(8,128)(2,1)}, bf16[16,144,128]{2,1,0:T(8,128)(2,1)S(1)}, u32[]{:S(2)}) %copy-start.5) | copy-done | bytes 589848
  18.9 22.4 %shard_map.56.own_ref = bf16[2,16,144,128]{3,2,1,0:T(8,128)(2,1)} custom-call(bf16[16,144,128]{2,1,0:T(8,128)(2,1)} %copy-done.5), custom_call_target="tpu_custom_call" | custom-call | tf_op jit(solution)/shard_map/pallas_call | solution.py:479
  41.3 0.1 copy.14.shift_ref
  41.5 1.1 %reshape.87.matrix_ref = bf16[8,144,144]{2,1,0:T(8,128)(2,1)S(1)} reshape(bf16[2,2,2,20736]{3,2,1,0:T(2,128)(2,1)S(1)} %copy-done.7) | data formatting | bytes 663552 | tf_op jit(solution)/shard_map/reshape | solution.py:523
  42.5 0.0 copy-done
  42.6 5.1 %shard_map.57.in_ref = bf16[16,144,128]{2,1,0:T(8,128)(2,1)S(1)} custom-call(bf16[2,16,144,128]{3,2,1,0:T(8,128)(2,1)S(1)} %copy-done, bf16[8,288,128]{2,1,0:T(8,128)(2,1)S(1)} %get-tuple-element.9.table_ref, f32[2,144,16]{2,1,0:T(8,128)S(1)} %copy.14.shift_ref, bf16[1152,1152]{1,0:T(8,128)(2,1)} %get-tuple-element.10.weight_ref, ...), custom_call_target="tpu_custom_call" | custom-call | tf_op jit(solution)/shard_map/pallas_call | solution.py:538
  47.7 0.0 copy-start.2
  47.7 0.8 %copy-done.2 = bf16[16,144,128]{2,1,0:T(8,128)(2,1)} copy-done((bf16[16,144,128]{2,1,0:T(8,128)(2,1)}, bf16[16,144,128]{2,1,0:T(8,128)(2,1)S(1)}, u32[]{:S(2)}) %copy-start.2) | copy-done | bytes 589848
  48.5 19.2 %shard_map.58.block_ref = bf16[16,144,128]{2,1,0:T(8,128)(2,1)} custom-call(bf16[16,144,128]{2,1,0:T(8,128)(2,1)} %copy-done.2), custom_call_target="tpu_custom_call" | custom-call | tf_op jit(solution)/shard_map/pallas_call | solution.py:479
  67.7 1.1 %copy-done.1 = bf16[16,144,128]{2,1,0:T(8,128)(2,1)S(1)} copy-done((bf16[16,144,128]{2,1,0:T(8,128)(2,1)S(1)}, bf16[16,144,128]{2,1,0:T(8,128)(2,1)}, u32[]{:S(2)}) %copy-start.1) | copy-done | bytes 589848
  68.8 1.6 %copy-done.3 = bf16[1024,1024]{1,0:T(8,128)(2,1)S(1)} copy-done((bf16[1024,1024]{1,0:T(8,128)(2,1)S(1)}, bf16[1024,1024]{1,0:T(8,128)(2,1)}, u32[]{:S(2)}) %copy-start.3) | copy-done | bytes 2097176
  70.4 1.7 %shard_map.59 = bf16[288,1024]{1,0:T(8,128)(2,1)} custom-call(bf16[16,144,128]{2,1,0:T(8,128)(2,1)S(1)} %copy-done.1, bf16[1024,1024]{1,0:T(8,128)(2,1)S(1)} %copy-done.3), custom_call_target="tpu_custom_call" | custom-call | tf_op jit(solution)/shard_map/pallas_call | solution.py:550
  (16 shorter events, 0.1 us)
Async XLA Ops:
  1.6 1.3 %copy-start.6 = (bf16[4,4,2,20736]{3,2,1,0:T(2,128)(2,1)S(1)}, bf16[4,4,2,20736]{3,2,1,0:T(2,128)(2,1)}, u32[]{:S(2)}) copy-start(bf16[4,4,2,20736]{3,2,1,0:T(2,128)(2,1)} %param.7) | copy-start | bytes 3981316
  3.0 5.6 %copy-start.4 = (bf16[288,1,1,1024]{3,0,2,1:T(8,128)(2,1)S(1)}, bf16[288,1,1,1024]{3,0,2,1:T(8,128)(2,1)}, u32[]{:S(2)}) copy-start(bf16[288,1,1,1024]{3,0,2,1:T(8,128)(2,1)} %param.5) | copy-start | bytes 1769476
  18.1 0.8 %copy-start.5 = (bf16[16,144,128]{2,1,0:T(8,128)(2,1)}, bf16[16,144,128]{2,1,0:T(8,128)(2,1)S(1)}, u32[]{:S(2)}) copy-start(bf16[16,144,128]{2,1,0:T(8,128)(2,1)S(1)} %get-tuple-element.8.in_ref) | copy-start | bytes 1769476
  18.9 22.5 %copy-start.7 = (bf16[2,2,2,20736]{3,2,1,0:T(2,128)(2,1)S(1)}, bf16[2,2,2,20736]{3,2,1,0:T(2,128)(2,1)}, u32[]{:S(2)}) copy-start(bf16[2,2,2,20736]{3,2,1,0:T(2,128)(2,1)} %param.8) | copy-start | bytes 995332
  41.3 1.3 %copy-start = (bf16[2,16,144,128]{3,2,1,0:T(8,128)(2,1)S(1)}, bf16[2,16,144,128]{3,2,1,0:T(8,128)(2,1)}, u32[]{:S(2)}) copy-start(bf16[2,16,144,128]{3,2,1,0:T(8,128)(2,1)} %shard_map.56.own_ref) | copy-start | bytes 3538948
  47.7 0.8 %copy-start.2 = (bf16[16,144,128]{2,1,0:T(8,128)(2,1)}, bf16[16,144,128]{2,1,0:T(8,128)(2,1)S(1)}, u32[]{:S(2)}) copy-start(bf16[16,144,128]{2,1,0:T(8,128)(2,1)S(1)} %shard_map.57.in_ref) | copy-start | bytes 1769476
  67.7 1.1 %copy-start.1 = (bf16[16,144,128]{2,1,0:T(8,128)(2,1)S(1)}, bf16[16,144,128]{2,1,0:T(8,128)(2,1)}, u32[]{:S(2)}) copy-start(bf16[16,144,128]{2,1,0:T(8,128)(2,1)} %shard_map.58.block_ref) | copy-start | bytes 1769476
  68.8 1.6 %copy-start.3 = (bf16[1024,1024]{1,0:T(8,128)(2,1)S(1)}, bf16[1024,1024]{1,0:T(8,128)(2,1)}, u32[]{:S(2)}) copy-start(bf16[1024,1024]{1,0:T(8,128)(2,1)} %constant.70.clone.order_ref) | copy-start | bytes 6291460

commit v2 on v1

--- a/solution.py
+++ b/solution.py
@@ -289,14 +289,13 @@
         table_out[block] = state[block, width : 2 * width, :]
 
 
-def far_kernel(
-    own_ref, table_ref, shift_ref, weight_ref, matrix_ref, out_ref, state, tables, other, pair_ref
-):
-    width = 2 * P_SIZE
-    assemble(matrix_ref, pair_ref, 2)
+def chip_of(y, x, z1, z0):
+    return y * 8 + x * 4 + z1 * 2 + z0
+
+
+def far_tables(table_ref, shift_ref, tables):
     half = lax.axis_index("gy") // 2 % 2
     chip = lax.axis_index("gx") * 4 + lax.axis_index("gy") // 2
-    core = lax.axis_index("gy") % 2
     lane = lax.broadcasted_iota(jnp.int32, (P_SIZE, LANES), 1)
     keep = (lane // 64) == half
     table = table_ref[chip // 2].astype(F32)
@@ -304,10 +303,6 @@
     for k in range(2):
         part = table[k * P_SIZE : (k + 1) * P_SIZE]
         base.append(jnp.where(keep, part, pltpu.roll(part, 64, 1)))
-
-    def chip_of(y, x, z1, z0):
-        return y * 8 + x * 4 + z1 * 2 + z0
-
     for y in range(2):
         for x in range(2):
             for z0 in range(2):
@@ -319,6 +314,15 @@
                     pick.append(jnp.where(lane < 64, low, high))
                 tables[block, 0] = base[0] * pick[0] - base[1] * pick[1]
                 tables[block, 1] = base[0] * pick[1] + base[1] * pick[0]
+
+
+def far_kernel(own_ref, weight_ref, pair_ref, out_ref, state, tables, other):
+    width = 2 * P_SIZE
+    core = lax.axis_index("gy") % 2
+    for y in range(2):
+        for x in range(2):
+            for z0 in range(2):
+                block = y * 4 + x * 2 + z0
                 for step in range(2):
                     low, high = swap_pair(
                         own_ref[step, chip_of(y, x, 0, z0)], own_ref[step, chip_of(y, x, 1, z0)], 64
@@ -400,58 +404,83 @@
         ).astype(BF16)
 
 
-def trade_kernel(both, in_ref, out_ref, send_sem, recv_sem, pass_send, pass_recv, own_sem):
+def whole_kernel(
+    source_ref,
+    table_ref,
+    matrix_ref,
+    shift_ref,
+    pairs_ref,
+    order_hbm,
+    image_ref,
+    blocks,
+    near_table,
+    weight,
+    near_state,
+    gathered,
+    state,
+    tables,
+    other,
+    pair_weight,
+    results,
+    returned,
+    home,
+    order,
+    send_sem,
+    recv_sem,
+    pass_send,
+    pass_recv,
+    back_send,
+    back_recv,
+    own_sem,
+):
     gx = lax.axis_index("gx")
     gy = lax.axis_index("gy")
     core = gy % 2
-    chip = gx * 4 + gy // 2
-    mate = (gx, gy // 2 * 2 + (1 - core))
+    zed = gy // 2
+    chip = gx * 4 + zed
+    mate = (gx, zed * 2 + (1 - core))
+    hops = [(1, a, b) for a in range(4) for b in range(2)]
+    hops += [(0, a, b) for a in range(4) for b in range(2) if a or b]
 
     def place(index):
         return (index // 4, index % 4 * 2 + core)
-
-    barrier = pltpu.get_barrier_semaphore()
-    for k in range(1, CHIPS):
-        pl.semaphore_signal(
-            barrier, inc=1, device_id=place((chip + k) % CHIPS), device_id_type=MESH_ID
-        )
-    if both:
-        pl.semaphore_signal(barrier, inc=1, device_id=mate, device_id_type=MESH_ID)
-    pl.semaphore_wait(barrier, CHIPS if both else CHIPS - 1)
-
-    def landing(which, index):
-        return out_ref.at[which, index] if both else out_ref.at[index]
-
-    far_first = [(1, a, b) for a in range(4) for b in range(2)]
-    far_first += [(0, a, b) for a in range(4) for b in range(2) if a or b]
-    zed = gy // 2
 
     def across(hop, back):
         other_half, a, b = hop
         x = (gx + (4 - a if back else a)) % 4
         return x * 4 + (zed // 2 + other_half) % 2 * 2 + (zed + b) % 2
 
-    sends = []
-    for k in range(1, CHIPS):
-        dest = across(far_first[k - 1], False)
-        copy = pltpu.make_async_remote_copy(
-            src_ref=in_ref.at[dest],
-            dst_ref=landing(0, chip),
-            send_sem=send_sem.at[k],
-            recv_sem=recv_sem.at[k],
-            device_id=place(dest),
-            device_id_type=MESH_ID,
-        )
-        copy.start()
-        sends.append(copy)
-    own = pltpu.make_async_copy(in_ref.at[chip], landing(0, chip), own_sem)
-    own.start()
-
-    def forward(k, src):
-        index = across(far_first[k - 1], True) if k else chip
+    barrier = pltpu.get_barrier_semaphore()
+    for hop in hops:
+        pl.semaphore_signal(
+            barrier, inc=1, device_id=place(across(hop, False)), device_id_type=MESH_ID
+        )
+    pl.semaphore_signal(barrier, inc=1, device_id=mate, device_id_type=MESH_ID)
+    order_copy = pltpu.make_async_copy(order_hbm, order, own_sem.at[2])
+    order_copy.start()
+    near_kernel(source_ref, table_ref, matrix_ref, blocks, near_table, weight, near_state)
+    pl.semaphore_wait(barrier, CHIPS)
+
+    def post(source, landing, send, recv):
+        copies = []
+        for k, hop in enumerate(hops):
+            dest = across(hop, False)
+            copy = pltpu.make_async_remote_copy(
+                src_ref=source.at[dest],
+                dst_ref=landing.at[chip],
+                send_sem=send.at[k],
+                recv_sem=recv.at[k],
+                device_id=place(dest),
+                device_id_type=MESH_ID,
+            )
+            copy.start()
+            copies.append(copy)
+        return copies
+
+    def forward(k, src, index):
         copy = pltpu.make_async_remote_copy(
             src_ref=src,
-            dst_ref=landing(1, index),
+            dst_ref=gathered.at[1, index],
             send_sem=pass_send.at[k],
             recv_sem=pass_recv.at[k],
             device_id=mate,
@@ -460,30 +489,30 @@
         copy.start()
         return copy
 
-    passes = []
-    if both:
-        passes.append(forward(0, in_ref.at[chip]))
-    for k in range(1, CHIPS):
-        sends[k - 1].wait_recv()
-        if both:
-            passes.append(forward(k, landing(0, across(far_first[k - 1], True))))
+    sends = post(blocks, gathered.at[0], send_sem, recv_sem)
+    own = pltpu.make_async_copy(blocks.at[chip], gathered.at[0, chip], own_sem.at[0])
+    own.start()
+    passes = [forward(15, blocks.at[chip], chip)]
+    assemble(pairs_ref, pair_weight, 2)
+    far_tables(near_table, shift_ref, tables)
+    for k, hop in enumerate(hops):
+        sends[k].wait_recv()
+        index = across(hop, True)
+        passes.append(forward(k, gathered.at[0, index], index))
+    own.wait()
+    for copy in passes:
+        copy.wait()
+    far_kernel(gathered, weight, pair_weight, results, state, tables, other)
+    backs = post(results, returned, back_send, back_recv)
+    own = pltpu.make_async_copy(results.at[chip], returned.at[chip], own_sem.at[1])
+    own.start()
+    order_copy.wait()
     own.wait()
     for copy in sends:
         copy.wait_send()
-    for copy in passes:
+    for copy in backs:
         copy.wait()
-
-
-def trade(blocks, both, identity):
-    shape = ((2,) if both else ()) + blocks.shape
-    return pl.pallas_call(
-        functools.partial(trade_kernel, both),
-        out_shape=jax.ShapeDtypeStruct(shape, BF16),
-        in_specs=[pl.BlockSpec(memory_space=pl.ANY)],
-        out_specs=pl.BlockSpec(memory_space=pl.ANY),
-        scratch_shapes=[pltpu.SemaphoreType.DMA((CHIPS,))] * 4 + [pltpu.SemaphoreType.DMA],
-        compiler_params=pltpu.CompilerParams(collective_id=identity, has_side_effects=True),
-    )(blocks)
+    home_kernel(returned, order, image_ref, home)
 
 
 def turned(angle):
@@ -522,37 +551,36 @@
     matrices = quad.reshape(32, P_SIZE, P_SIZE)
     pairs = pair.reshape(8, P_SIZE, P_SIZE)
     order = jnp.asarray(home_columns()[:, None] == np.arange(SIDE * SIDE)[None], BF16)
-    roomy = pltpu.CompilerParams(vmem_limit_bytes=50 * 1024 * 1024)
-    block_shape = jax.ShapeDtypeStruct((CHIPS, P_SIZE, LANES), BF16)
-    blocks, near_table, weight = pl.pallas_call(
-        near_kernel,
-        out_shape=(
-            block_shape,
-            jax.ShapeDtypeStruct((8, width_all, LANES), BF16),
-            jax.ShapeDtypeStruct((4 * width_all, 4 * width_all), BF16),
-        ),
-        scratch_shapes=[pltpu.VMEM((8, 2 * width_all, LANES), BF16)],
-        compiler_params=roomy,
-    )(source.reshape(width_all, SIDE * SIDE), table, matrices)
-    gathered = trade(blocks, True, 0)
-    results = pl.pallas_call(
-        far_kernel,
-        out_shape=block_shape,
+    vmem = pl.BlockSpec(memory_space=pltpu.VMEM)
+    tile = (P_SIZE, LANES)
+    size = SIDE * SIDE
+    dma = pltpu.SemaphoreType.DMA
+    image = pl.pallas_call(
+        whole_kernel,
+        out_shape=jax.ShapeDtypeStruct((width_all, size), BF16),
+        in_specs=[vmem] * 5 + [pl.BlockSpec(memory_space=pl.ANY)],
+        out_specs=vmem,
         scratch_shapes=[
+            pltpu.VMEM((CHIPS,) + tile, BF16),
             pltpu.VMEM((8, width_all, LANES), BF16),
-            pltpu.VMEM((8, 2, P_SIZE, LANES), F32),
+            pltpu.VMEM((4 * width_all, 4 * width_all), BF16),
+            pltpu.VMEM((8, 2 * width_all, LANES), BF16),
+            pltpu.VMEM((2, CHIPS) + tile, BF16),
+            pltpu.VMEM((8, width_all, LANES), BF16),
+            pltpu.VMEM((8, 2) + tile, F32),
             pltpu.VMEM((8, width_all, LANES), BF16),
             pltpu.VMEM((2 * width_all, 2 * width_all), BF16),
-        ],
-        compiler_params=roomy,
-    )(gathered, near_table, shift, weight, pairs)
-    returned = trade(results, False, 1)
-    image = pl.pallas_call(
-        home_kernel,
-        out_shape=jax.ShapeDtypeStruct((width_all, SIDE * SIDE), BF16),
-        scratch_shapes=[pltpu.VMEM((width_all, SIDE * SIDE), BF16)],
-        compiler_params=roomy,
-    )(returned, order)
+            pltpu.VMEM((CHIPS,) + tile, BF16),
+            pltpu.VMEM((CHIPS,) + tile, BF16),
+            pltpu.VMEM((width_all, size), BF16),
+            pltpu.VMEM((size, size), BF16),
+        ]
+        + [dma((CHIPS,))] * 6
+        + [dma((3,))],
+        compiler_params=pltpu.CompilerParams(
+            collective_id=0, has_side_effects=True, vmem_limit_bytes=50 * 1024 * 1024
+        ),
+    )(source.reshape(width_all, size), table, matrices, shift, pairs, order)
     return image.reshape(width_all, 1, 1, SIDE * SIDE)
 
 

time: 72.4 us -> 60.3 us (0.83)
  Pallas kernels: 57.9 us -> 48.6 us
  local copies, waits for them, and re-layouts: 13.1 us -> 10.5 us
    pallas_call x5 -> x1, Pallas kernels: 57.9 us -> 48.6 us  [traded(): pl.pallas_call(whole_kernel, out_shape=jax.ShapeDtypeStruct((width_all, s...]
    unnamed x16 -> x5, local copies, waits for them, and re-layouts: 5.21 us -> 1.74 us
    reshape x1, local copies, waits for them, and re-layouts: 1.08 us -> 1.89 us  [traded(): pairs = pair.reshape(8, P_SIZE, P_SIZE)]
where the time goes in v2:
time: 60.3 us; the launch traced here: 60 us
  Pallas kernels  48.6 us (81%)
  local copies, waits for them, and re-layouts  10.5 us (17%)
  other arithmetic  0.86 us (1%)
    pallas_call x1, Pallas kernels, traded(): pl.pallas_call(whole_kernel, out_shape=jax.ShapeDtypeStruct((width_all, s...  48.6 us
    reshape x1, local copies, waits for them, and re-layouts, traded(): matrices = quad.reshape(32, P_SIZE, P_SIZE)  5.61 us
    reshape x1, local copies, waits for them, and re-layouts, traded(): pairs = pair.reshape(8, P_SIZE, P_SIZE)  1.89 us
    unnamed x5, local copies, waits for them, and re-layouts  1.74 us

profile of v2, /device:TPU:0, one launch (start us, length us, event | category | flops | bytes accessed | tf_op | source)
XLA Modules:
  0.0 60.0 jit_solution(16711831923415793158)
XLA Ops:
  0.0 0.8 %fusion.14 = (f32[1,144]{1,0:T(1,128)S(1)}, f32[1,144]{1,0:T(1,128)S(1)}) fusion(f32[2,144]{1,0:T(2,128)} %param.6), kind=kLoop, calls=%fused_computation.31 | loop fusion | bytes 2304 | tf_op jit(solution)/shard_map/slice | solution.py:539
  0.8 0.1 multiply_add_fusion
  0.9 0.1 broadcast_multiply_fusion
  0.9 0.3 fusion.1
  1.3 0.1 copy.14.shift_ref
  1.4 1.9 %reshape.87.pairs_ref = bf16[8,144,144]{2,1,0:T(8,128)(2,1)S(1)} reshape(bf16[2,2,2,20736]{3,2,1,0:T(2,128)(2,1)} %param.8) | data formatting | bytes 663552 | tf_op jit(solution)/shard_map/reshape | solution.py:552
  3.3 0.3 subtract_convert_fusion
  3.7 0.0 copy-start.1
  3.7 0.2 copy.12
  3.9 0.2 copy.13
  4.1 0.9 %copy-done.1 = bf16[4,4,2,20736]{3,2,1,0:T(2,128)(2,1)S(1)} copy-done((bf16[4,4,2,20736]{3,2,1,0:T(2,128)(2,1)S(1)}, bf16[4,4,2,20736]{3,2,1,0:T(2,128)(2,1)}, u32[]{:S(2)}) %copy-start.1) | copy-done | bytes 1327128
  5.0 0.0 copy-start
  5.0 5.6 %reshape.86.matrix_ref = bf16[32,144,144]{2,1,0:T(8,128)(2,1)} reshape(bf16[4,4,2,20736]{3,2,1,0:T(2,128)(2,1)S(1)} %copy-done.1) | data formatting | bytes 2654208 | tf_op jit(solution)/shard_map/reshape | solution.py:551
  10.6 0.0 copy-done
  10.6 48.6 %shard_map.55 = bf16[288,1024]{1,0:T(8,128)(2,1)S(1)} custom-call(bf16[288,1024]{1,0:T(8,128)(2,1)S(1)} %bitcast.11, bf16[288,1024]{1,0:T(8,128)(2,1)S(1)} %pad_maximum_fusion.table_ref, bf16[32,144,144]{2,1,0:T(8,128)(2,1)} %reshape.86.matrix_ref, f32[2,144,16]{2,1,0:T(8,128)S(1)} %copy.14.shift_ref, bf16[8,144,144]{2,1,0:T(8,128)(2,1)S(1)} %reshape.87.pairs_ref, ...), custom_call_target="tpu_custom_call" | custom-call | tf_op jit(solution)/shard_map/pallas_call | solution.py:558
  59.2 0.8 %copy.16 = bf16[288,1,1,1024]{3,0,2,1:T(8,128)(2,1)} copy(bf16[288,1,1,1024]{3,0,2,1:T(8,128)(2,1)S(1)} %bitcast.10) | data formatting | bytes 1179648
  (9 shorter events, 0.1 us)
Async XLA Ops:
  3.7 1.3 %copy-start.1 = (bf16[4,4,2,20736]{3,2,1,0:T(2,128)(2,1)S(1)}, bf16[4,4,2,20736]{3,2,1,0:T(2,128)(2,1)}, u32[]{:S(2)}) copy-start(bf16[4,4,2,20736]{3,2,1,0:T(2,128)(2,1)} %param.7) | copy-start | bytes 3981316
  5.0 5.6 %copy-start = (bf16[288,1,1,1024]{3,0,2,1:T(8,128)(2,1)S(1)}, bf16[288,1,1,1024]{3,0,2,1:T(8,128)(2,1)}, u32[]{:S(2)}) copy-start(bf16[288,1,1,1024]{3,0,2,1:T(8,128)(2,1)} %param.5) | copy-start | bytes 1769476
